TPU v7x, 128 devices: a whole 4x4x4 slice. The times are simulated.
128 devices in a mesh: lat: 8 (over x, z_hi), lon: 16 (over z_lo, y, core).
Axes of the slice: x: 4, y: 4, z: 4 (z_hi: 2, z_lo: 2; z = z_hi * 2 + z_lo), core: 2. Of those that a mesh axis runs over, the one named last changes fastest.
Arguments:
- tokens: bfloat16 [1, 96, 384, 512], P(None, 'lat', 'lon'), may hold values from -6 to 6
- qkv_first: bfloat16 [1536, 512], replicated, may hold values from -1 to 1, as said below
- out_first: bfloat16 [512, 512], replicated, may hold values from -0.25 to 0.25
- qkv_second: bfloat16 [1536, 512], replicated, may hold values from -1 to 1, as said below
- out_second: bfloat16 [512, 512], replicated, may hold values from -0.25 to 0.25
- merge_weight: bfloat16 [1024, 2048], replicated, may hold values from -0.125 to 0.125
- qkv_third: bfloat16 [3072, 1024], replicated, may hold values from -1 to 1, as said below
- out_third: bfloat16 [1024, 1024], replicated, may hold values from -0.1875 to 0.1875
- cotangent: bfloat16 [1, 48, 192, 1024], P(None, 'lat', 'lon'), may hold values from -6 to 6
Outputs:
- latent: bfloat16 [1, 48, 192, 1024], P(None, 'lat', 'lon')
- tokens_grad: bfloat16 [1, 96, 384, 512], P(None, 'lat', 'lon')
- qkv_first_grad: float32 [1536, 512], P(('lat', 'lon'))
- out_first_grad: float32 [512, 512], P(('lat', 'lon'))
- qkv_second_grad: float32 [1536, 512], P(('lat', 'lon'))
- out_second_grad: float32 [512, 512], P(('lat', 'lon'))
- merge_grad: float32 [1024, 2048], P(('lat', 'lon'))
- qkv_third_grad: float32 [3072, 1024], P(('lat', 'lon'))
- out_third_grad: float32 [1024, 1024], P(('lat', 'lon'))
Inputs may be any that keep to these rules, and one draw needn't show every extreme that they name: `qkv_first`: a query, key and value projection, query and key rows first. `qkv_second`: a query, key and value projection, query and key rows first. `qkv_third`: a query, key and value projection, query and key rows first.
All inputs are finite; a program needn't handle non-finite values.
Results may differ from a plain program's by a relative error of at most 0.04.
Values may be sent and summed in bfloat16 or wider, within the bound.
No kernel may reach another device: no remote copies, remote signals or barrier semaphores. Data moves between devices by JAX's collectives and lax.ppermute only.
A program may use at most 192 MiB of HBM per device.

v0:
```python
import jax
import jax.numpy as jnp
from jax import lax
from jax.sharding import PartitionSpec as P

HDIM = 64
LEV = 1
WA = 6
WO = 12


EPSILON = 1e-05


def from_behind(block, axis, distance):
    devices = range(lax.axis_size(axis))
    route = [((i - distance) % len(devices), i) for i in devices]
    return lax.ppermute(block, axis, route)


def normalize(field):
    values = field.astype(jnp.float32)
    average = jnp.mean(values, axis=-1, keepdims=True)
    centered = values - average
    variance = jnp.mean(centered * centered, axis=-1, keepdims=True)
    return (centered * lax.rsqrt(variance + EPSILON)).astype(jnp.bfloat16)


def project(rows, matrix):
    return lax.dot_general(
        rows, matrix, (((1,), (1,)), ((), ())), preferred_element_type=jnp.float32
    )


def grad_weight(cotan, rows):
    return lax.dot_general(
        cotan, rows, (((0,), (0,)), ((), ())), preferred_element_type=jnp.float32
    )


def pull_back(cotan, matrix):
    return jnp.dot(cotan, matrix, preferred_element_type=jnp.float32).astype(jnp.bfloat16)


def combine(first_term, second_term):
    return (first_term.astype(jnp.float32) + second_term.astype(jnp.float32)).astype(jnp.bfloat16)


def windows(field, lat_win, lon_win):
    levels, lat_rows, lon_cols, channels = field.shape
    blocked = field.reshape(
        levels, lat_rows // lat_win, lat_win, lon_cols // lon_win, lon_win, channels
    )
    blocked = blocked.transpose(1, 3, 0, 2, 4, 5)
    return blocked.reshape(
        lat_rows // lat_win * (lon_cols // lon_win), levels * lat_win * lon_win, channels
    )


def unwindows(blocks, grid_shape, lat_win, lon_win):
    levels, lat_rows, lon_cols, channels = grid_shape
    blocked = blocks.reshape(
        lat_rows // lat_win, lon_cols // lon_win, levels, lat_win, lon_win, channels
    )
    blocked = blocked.transpose(2, 0, 3, 1, 4, 5)
    return blocked.reshape(levels, lat_rows, lon_cols, channels)


def merge_patches(field):
    levels, lat_rows, lon_cols, channels = field.shape
    blocked = field.reshape(levels, lat_rows // 2, 2, lon_cols // 2, 2, channels).transpose(
        0, 1, 3, 4, 2, 5
    )
    return blocked.reshape(levels, lat_rows // 2, lon_cols // 2, 4 * channels)


def split_patches(field):
    levels, lat_half, lon_half, four_channels = field.shape
    blocked = field.reshape(levels, lat_half, lon_half, 2, 2, four_channels // 4).transpose(
        0, 1, 4, 2, 3, 5
    )
    return blocked.reshape(levels, 2 * lat_half, 2 * lon_half, four_channels // 4)


def region_bias(rows_start, lat_total, grid_shape, lat_win, lon_win):
    levels, lat_rows, lon_cols, channels = grid_shape
    row_index = rows_start + jnp.arange(lat_rows, dtype=jnp.int32)
    region = (row_index >= lat_total - lat_win).astype(jnp.float32) + (
        row_index >= lat_total - lat_win // 2
    ).astype(jnp.float32)
    region_grid = jnp.broadcast_to(region[None, :, None, None], (levels, lat_rows, lon_cols, 1))
    region_tags = windows(region_grid, lat_win, lon_win)[:, :, 0]
    same = region_tags[:, :, None] == region_tags[:, None, :]
    return jnp.where(same, jnp.float32(0.0), jnp.float32(-1e30))


def split_product(form, wide, narrow):
    upper = wide.astype(jnp.bfloat16)
    lower = (wide - upper.astype(jnp.float32)).astype(jnp.bfloat16)
    first_part = jnp.einsum(form, upper, narrow, preferred_element_type=jnp.float32)
    return first_part + jnp.einsum(form, lower, narrow, preferred_element_type=jnp.float32)


def attend_forward(packed, mask_bias):
    window_count, window_size, triple_width = packed.shape
    channels = triple_width // 3
    head_count = channels // HDIM
    scale = HDIM ** (-0.5)
    unpacked = packed.reshape(window_count, window_size, 3, head_count, HDIM)
    queries = unpacked[:, :, 0]
    keys_all = unpacked[:, :, 1]
    values_all = unpacked[:, :, 2]
    scores = jnp.einsum("wqhd,wkhd->whqk", queries, keys_all, preferred_element_type=jnp.float32)
    scores = scores * scale + mask_bias[:, None]
    probs = jax.nn.softmax(scores, axis=-1)
    weights = probs.astype(jnp.bfloat16)
    blended = jnp.einsum("whqk,wkhd->wqhd", weights, values_all, preferred_element_type=jnp.float32)
    blended = blended.reshape(window_count, window_size, channels).astype(jnp.bfloat16)

    def core_back(cotan):
        cotan_heads = cotan.reshape(window_count, window_size, head_count, HDIM)
        cotan_weights = jnp.einsum(
            "wqhd,wkhd->whqk", cotan_heads, values_all, preferred_element_type=jnp.float32
        )
        cotan_weights = cotan_weights.astype(jnp.bfloat16).astype(jnp.float32)
        inner = jnp.sum(probs * cotan_weights, axis=-1, keepdims=True)
        cotan_scores = probs * (cotan_weights - inner) * scale
        cotan_queries = split_product("whqk,wkhd->wqhd", cotan_scores, keys_all)
        cotan_keys = split_product("whqk,wqhd->wkhd", cotan_scores, queries)
        cotan_values = jnp.einsum(
            "whqk,wqhd->wkhd", weights, cotan_heads, preferred_element_type=jnp.float32
        )
        stacked = jnp.stack(
            [
                cotan_queries.astype(jnp.bfloat16),
                cotan_keys.astype(jnp.bfloat16),
                cotan_values.astype(jnp.bfloat16),
            ],
            axis=2,
        )
        return (stacked.reshape(window_count, window_size, triple_width),)

    return (blended, core_back)


def attention_forward(field, w_qkv, w_out, mask_bias, lat_win, lon_win):
    normed, norm_back = jax.vjp(normalize, field)
    blocks = windows(normed, lat_win, lon_win)
    window_count, window_size, channels = blocks.shape
    flat_rows = blocks.reshape(window_count * window_size, channels)
    triple = (
        project(flat_rows, w_qkv)
        .astype(jnp.bfloat16)
        .reshape(window_count, window_size, 3 * channels)
    )
    blended, core_back = attend_forward(triple, mask_bias)
    blended_flat = blended.reshape(window_count * window_size, channels)
    result = project(blended_flat, w_out).astype(jnp.bfloat16)
    result = unwindows(
        result.reshape(window_count, window_size, channels), field.shape, lat_win, lon_win
    )
    return (result, (flat_rows, blended_flat, norm_back, core_back))


def attention_backward(cotan, stored, w_qkv, w_out, grid_shape, lat_win, lon_win):
    flat_rows, blended_flat, norm_back, core_back = stored
    blocks = windows(cotan, lat_win, lon_win)
    window_count, window_size, channels = blocks.shape
    cotan_flat = blocks.reshape(window_count * window_size, channels)
    grad_out = grad_weight(cotan_flat, blended_flat)
    cotan_blended = pull_back(cotan_flat, w_out).reshape(window_count, window_size, channels)
    (cotan_triple,) = core_back(cotan_blended)
    triple_flat = cotan_triple.reshape(window_count * window_size, 3 * channels)
    grad_qkv = grad_weight(triple_flat, flat_rows)
    cotan_normed = pull_back(triple_flat, w_qkv).reshape(window_count, window_size, channels)
    (cotan_field,) = norm_back(unwindows(cotan_normed, grid_shape, lat_win, lon_win))
    return (cotan_field, (grad_qkv, grad_out))


def roll_ahead(field):
    half_lat = WA // 2
    half_lon = WO // 2
    incoming = from_behind(field[:, :half_lat], "lat", -1)
    field = jnp.concatenate([field[:, half_lat:], incoming], axis=1)
    incoming = from_behind(field[:, :, :half_lon], "lon", -1)
    return jnp.concatenate([field[:, :, half_lon:], incoming], axis=2)


def roll_behind(field):
    half_lat = WA // 2
    half_lon = WO // 2
    incoming = from_behind(field[:, -half_lat:], "lat", 1)
    field = jnp.concatenate([incoming, field[:, :-half_lat]], axis=1)
    incoming = from_behind(field[:, :, -half_lon:], "lon", 1)
    return jnp.concatenate([incoming, field[:, :, :-half_lon]], axis=2)


def on_device(
    tokens,
    qkv_first,
    out_first,
    qkv_second,
    out_second,
    merge_weight,
    qkv_third,
    out_third,
    cotangent,
):
    grid_shape = tokens.shape
    span = LEV * WA * WO
    no_bias = jnp.zeros((1, span, span), jnp.float32)
    first_out, first_store = attention_forward(tokens, qkv_first, out_first, no_bias, WA, WO)
    layer_one = combine(tokens, first_out)
    rolled = roll_ahead(layer_one)
    tile_rows = grid_shape[1]
    mask_bias = region_bias(
        lax.axis_index("lat") * tile_rows, tile_rows * lax.axis_size("lat"), grid_shape, WA, WO
    )
    second_out, second_store = attention_forward(rolled, qkv_second, out_second, mask_bias, WA, WO)
    layer_two = combine(layer_one, roll_behind(second_out))
    merged = merge_patches(layer_two)
    normed, norm_back = jax.vjp(normalize, merged)
    merged_shape = normed.shape
    merged_rows = normed.reshape(-1, merged_shape[3])
    hidden = project(merged_rows, merge_weight).astype(jnp.bfloat16)
    hidden = hidden.reshape(merged_shape[0], merged_shape[1], merged_shape[2], -1)
    third_out, third_store = attention_forward(hidden, qkv_third, out_third, no_bias, WA, WO)
    latent = combine(hidden, third_out)
    third_cotan, third_grads = attention_backward(
        cotangent, third_store, qkv_third, out_third, hidden.shape, WA, WO
    )
    hidden_cotan = combine(cotangent, third_cotan)
    hidden_rows = hidden_cotan.reshape(-1, hidden.shape[3])
    merge_grad = grad_weight(hidden_rows, merged_rows)
    normed_cotan = pull_back(hidden_rows, merge_weight).reshape(merged_shape)
    (merged_cotan,) = norm_back(normed_cotan)
    two_cotan = split_patches(merged_cotan)
    second_cotan = roll_ahead(two_cotan)
    rolled_cotan, second_grads = attention_backward(
        second_cotan, second_store, qkv_second, out_second, grid_shape, WA, WO
    )
    one_cotan = combine(two_cotan, roll_behind(rolled_cotan))
    first_cotan, first_grads = attention_backward(
        one_cotan, first_store, qkv_first, out_first, grid_shape, WA, WO
    )
    tokens_grad = combine(one_cotan, first_cotan)
    shares = (
        lax.psum_scatter(first_grads[0], ("lat", "lon"), scatter_dimension=0, tiled=True),
        lax.psum_scatter(first_grads[1], ("lat", "lon"), scatter_dimension=0, tiled=True),
        lax.psum_scatter(second_grads[0], ("lat", "lon"), scatter_dimension=0, tiled=True),
        lax.psum_scatter(second_grads[1], ("lat", "lon"), scatter_dimension=0, tiled=True),
        lax.psum_scatter(merge_grad, ("lat", "lon"), scatter_dimension=0, tiled=True),
        lax.psum_scatter(third_grads[0], ("lat", "lon"), scatter_dimension=0, tiled=True),
        lax.psum_scatter(third_grads[1], ("lat", "lon"), scatter_dimension=0, tiled=True),
    )
    return (
        latent,
        tokens_grad,
        shares[0],
        shares[1],
        shares[2],
        shares[3],
        shares[4],
        shares[5],
        shares[6],
    )


def solution(mesh):
    placed = (
        P(None, "lat", "lon", None),
        P(),
        P(),
        P(),
        P(),
        P(),
        P(),
        P(),
        P(None, "lat", "lon", None),
    )
    return jax.shard_map(
        on_device,
        mesh=mesh,
        in_specs=placed,
        out_specs=(
            P(None, "lat", "lon", None),
            P(None, "lat", "lon", None),
            P(("lat", "lon"), None),
            P(("lat", "lon"), None),
            P(("lat", "lon"), None),
            P(("lat", "lon"), None),
            P(("lat", "lon"), None),
            P(("lat", "lon"), None),
            P(("lat", "lon"), None),
        ),
        check_vma=False,
    )
```

profile of v0, /device:TPU:0, one launch (start us, length us, event | category | flops | bytes accessed | tf_op | source)
XLA Modules:
  0.0 1921.0 jit_solution(6276875622630855232)
XLA Ops:
  39.1 6.2 collective-permute-start
  103.2 4.4 collective-permute-done.2
  112.3 4.1 collective-permute-done.3
  124.8 4.6 fusion.168
  134.1 5.7 convolution_convert_fusion
  163.6 5.2 multiply_reduce_fusion.6
  207.3 3.9 fusion.30
  211.2 3.9 fusion.29
  234.2 6.8 collective-permute-done.6
  242.9 5.2 collective-permute-done.7
  256.5 5.4 copy.296
  263.1 4.5 convolution_bitcast_fusion
  268.8 6.4 fusion.154
  285.6 4.0 fusion.76
  289.6 4.2 fusion.28
  297.6 4.0 fusion.27
  305.2 3.9 copy.274
  312.7 4.0 fusion.170
  316.7 364.7 %fusion.156 = (f32[16,512]{1,0:T(8,128)S(1)}, f32[16,512]{1,0:T(8,128)S(1)}) fusion(f32[1536,512]{1,0:T(8,128)} %fusion.170, f32[1536,512]{1,0:T(8,128)S(1)} %fusion.172), kind=kCustom, calls=%all-reduce-scatter.2 | all-reduce-scatter fusion | flops 2097153 | bytes 6356992
  684.0 5.8 collective-permute-start.71
  692.8 7.3 collective-permute-start.36
  712.1 6.2 collective-permute-start.30
  744.2 4.6 collective-permute-start.19
  765.1 4.6 collective-permute-start.11
  802.4 4.3 multiply_reduce_fusion
  828.3 5.0 fusion.157
  849.2 4.9 collective-permute-start.43
  863.6 26.0 %concatenate.68 = f32[524,512]{1,0:T(8,128)S(1)} concatenate(f32[12,512]{1,0:T(8,128)} %copy-done.63, f32[16,512]{1,0:T(8,128)S(1)} %copy-done.61, f32[16,512]{1,0:T(8,128)} %copy-done.62, f32[16,512]{1,0:T(8,128)} %copy-done.64, f32[16,512]{1,0:T(8,128)} %copy-done.65, f32[16,512]{1,0:T(8,128)} %copy-done.66, f32[16,512]{1,0:T(8,128)} %copy-done.67, f32[16,512]{1,0:T(8,128)} %copy-done.68, ...), dimensions={0} | concatenate | bytes 2146304
  889.8 45.9 %concatenate.69 = f32[524,512]{1,0:T(8,128)} concatenate(f32[12,512]{1,0:T(8,128)S(1)} %copy-done.59, f32[16,512]{1,0:T(8,128)S(1)} %copy-done.92, f32[16,512]{1,0:T(8,128)S(1)} %copy-done.96, f32[16,512]{1,0:T(8,128)S(1)} %copy-done.98, f32[16,512]{1,0:T(8,128)S(1)} %copy-done.100, f32[16,512]{1,0:T(8,128)S(1)} %copy-done.102, f32[16,512]{1,0:T(8,128)S(1)} %copy-done.104, ...), dimensions={0} | concatenate | bytes 2146304
  939.0 107.5 %reduce-scatter.14.cloned.1.call-done = f32[8,1024]{1,0:T(8,128)} async-done(((f32[1024,1024]{1,0:T(8,128)}), f32[8,1024]{1,0:T(8,128)}) %reduce-scatter.14.cloned.1.call-update) | async-done | bytes 32784
  1046.5 647.1 %reduce-scatter.10.cloned.1.call-done = f32[8,2048]{1,0:T(8,128)} async-done(((f32[1024,2048]{1,0:T(8,128)}), f32[8,2048]{1,0:T(8,128)}) %reduce-scatter.10.cloned.1.call-update) | async-done | bytes 65552 | tf_op jit(solution)/shard_map/reduce_scatter | solution.py:252
  1693.6 220.7 %reduce-scatter.12.cloned.1.call-done = f32[24,1024]{1,0:T(8,128)} async-done(((f32[3072,1024]{1,0:T(8,128)}), f32[24,1024]{1,0:T(8,128)}) %reduce-scatter.12.cloned.1.call-update) | async-done | bytes 98320 | tf_op jit(solution)/shard_map/reduce_scatter | solution.py:253
  (616 shorter events, 362.9 us)
Async XLA Ops:
  7.2 930.5 %all-reduce.10.cloned.1.call-start = ((), (), s32[]{:S(2)}) async-start(), calls=%async_computation.6 | async-start | bytes 4194304
  252.8 793.7 %reduce-scatter.14.cloned.1.call-start = ((), (), s32[]{:S(2)}) async-start(), calls=%async_computation.5 | async-start | bytes 4227072
  261.9 1431.7 %reduce-scatter.10.cloned.1.call-start = ((), (), s32[]{:S(2)}) async-start(), calls=%async_computation.3 | async-start | bytes 8454144 | tf_op jit(solution)/shard_map/reduce_scatter | solution.py:252
  267.6 1646.6 %reduce-scatter.12.cloned.1.call-start = ((), (), s32[]{:S(2)}) async-start(), calls=%async_computation.4 | async-start | bytes 12681216 | tf_op jit(solution)/shard_map/reduce_scatter | solution.py:253
  681.4 24.8 %collective-permute-start.38 = (f32[16,512]{1,0:T(8,128)S(1)}, f32[16,512]{1,0:T(8,128)S(1)}, u32[]{:S(2)}, u32[]{:S(2)}) collective-permute-start(f32[16,512]{1,0:T(8,128)S(1)} %get-tuple-element.58), channel_id=1, source_target_pairs={{0,31},{1,32},{2,33},{3,34},{4,35},{5,36},{6,37},{7,38},{8,39},{9,... | collective-permute-start | bytes 98312
  682.7 25.9 %collective-permute-start.37 = (f32[16,512]{1,0:T(8,128)S(1)}, f32[16,512]{1,0:T(8,128)S(1)}, u32[]{:S(2)}, u32[]{:S(2)}) collective-permute-start(f32[16,512]{1,0:T(8,128)S(1)} %get-tuple-element.58), channel_id=1, source_target_pairs={{0,30},{1,31},{2,32},{3,33},{4,34},{5,35},{6,36},{7,37},{8,38},{9,... | collective-permute-start | bytes 98312
  684.0 16.1 collective-permute-start.71
  692.8 18.0 collective-permute-start.36
  703.4 14.9 collective-permute-start.34
  706.3 15.1 collective-permute-start.33
  708.6 15.1 collective-permute-start.32
  710.8 16.0 collective-permute-start.31
  712.1 16.0 collective-permute-start.30
  754.3 15.4 collective-permute-start.15
  790.2 16.5 collective-permute-start.64
  791.5 16.9 collective-permute-start.63
  792.8 17.2 collective-permute-start.62
  796.1 16.1 collective-permute-start.61
  799.3 14.9 collective-permute-start.60
  816.8 16.5 collective-permute-start.54
  818.7 16.6 collective-permute-start.53
  820.8 17.2 collective-permute-start.52
  823.5 16.8 collective-permute-start.51
  826.9 17.2 collective-permute-start.50
  837.9 16.2 collective-permute-start.47
  840.4 15.7 collective-permute-start.46
  844.2 14.0 collective-permute-start.45
  846.1 43.5 %collective-permute-start.44 = (f32[16,512]{1,0:T(8,128)S(1)}, f32[16,512]{1,0:T(8,128)}, u32[]{:S(2)}, u32[]{:S(2)}) collective-permute-start(f32[16,512]{1,0:T(8,128)S(1)} %get-tuple-element.59), channel_id=1, source_target_pairs={{0,5},{1,6},{2,7},{3,8},{4,9},{5,10},{6,11},{7,12},{8,13},{9,14},{... | collective-permute-start | bytes 98312
  849.2 40.4 %collective-permute-start.43 = (f32[16,512]{1,0:T(8,128)S(1)}, f32[16,512]{1,0:T(8,128)}, u32[]{:S(2)}, u32[]{:S(2)}) collective-permute-start(f32[16,512]{1,0:T(8,128)S(1)} %get-tuple-element.59), channel_id=1, source_target_pairs={{0,4},{1,5},{2,6},{3,7},{4,8},{5,9},{6,10},{7,11},{8,12},{9,13},{1... | collective-permute-start | bytes 98312
  854.1 35.5 %collective-permute-start.42 = (f32[16,512]{1,0:T(8,128)S(1)}, f32[16,512]{1,0:T(8,128)}, u32[]{:S(2)}, u32[]{:S(2)}) collective-permute-start(f32[16,512]{1,0:T(8,128)S(1)} %get-tuple-element.59), channel_id=1, source_target_pairs={{0,3},{1,4},{2,5},{3,6},{4,7},{5,8},{6,9},{7,10},{8,11},{9,12},{10... | collective-permute-start | bytes 98312
  856.0 33.7 %collective-permute-start.41 = (f32[16,512]{1,0:T(8,128)S(1)}, f32[16,512]{1,0:T(8,128)}, u32[]{:S(2)}, u32[]{:S(2)}) collective-permute-start(f32[16,512]{1,0:T(8,128)S(1)} %get-tuple-element.59), channel_id=1, source_target_pairs={{0,2},{1,3},{2,4},{3,5},{4,6},{5,7},{6,8},{7,9},{8,10},{9,11},{10,... | collective-permute-start | bytes 98312
  858.2 31.5 %collective-permute-start.40 = (f32[16,512]{1,0:T(8,128)S(1)}, f32[16,512]{1,0:T(8,128)}, u32[]{:S(2)}, u32[]{:S(2)}) collective-permute-start(f32[16,512]{1,0:T(8,128)S(1)} %get-tuple-element.59), channel_id=1, source_target_pairs={{0,1},{1,2},{2,3},{3,4},{4,5},{5,6},{6,7},{7,8},{8,9},{9,10},{10,1... | collective-permute-start | bytes 98312
  (195 other events, 4225.9 us)
Sparse Core Ops, SparseCore 0:
  252.9 147.6 all-reduce.9
  403.6 642.8 reduce-scatter.13
  1049.6 643.9 reduce-scatter.9
  1699.0 215.1 reduce-scatter.11
where the time goes:
time: 1940 us; the launch traced here: 1920 us
  waiting for transfers between devices  1010 us (52%)
  blocking collectives  365 us (19%)
  starting transfers between devices  183 us (9%)
  local copies, waits for them, and re-layouts  174 us (9%)
  matrix products  130 us (7%)
  other arithmetic  47.1 us (2%)
    reduce_scatter x1, waiting for transfers between devices, on_device(): lax.psum_scatter(merge_grad, ('lat', 'lon'), scatter_dimension=0, tiled=T...  647 us
    unnamed x1, blocking collectives  365 us
    reduce_scatter x1, waiting for transfers between devices, on_device(): lax.psum_scatter(third_grads[0], ('lat', 'lon'), scatter_dimension=0, til...  221 us
    unnamed x66, starting transfers between devices  166 us
    unnamed x70, waiting for transfers between devices  108 us
    unnamed x317, local copies, waits for them, and re-layouts  103 us
  transfers between devices with their start and end apart: 76, of which 11 were waited for; matrix products, arithmetic and copies ran while one was open for 27% of the time, Pallas kernels for 0%

commit v1 on v0

v1 whole, which is shorter than its diff:
```python
import functools

import jax
import jax.numpy as jnp
import numpy as np
from jax import lax
from jax.experimental import pallas as pl
from jax.experimental.pallas import tpu as pltpu
from jax.sharding import Mesh, PartitionSpec as P

F32 = jnp.float32
BF16 = jnp.bfloat16
HDIM = 64
PAIR = 2 * HDIM
SCALE = HDIM ** (-0.5)
WA = 6
WO = 12
ROWS = 12
COLS = 24
TOK = ROWS * COLS
BAND = WA * COLS
C1 = 512
C2 = 1024
M_ROWS = 6
M_COLS = 12
M_TOK = M_ROWS * M_COLS
M_PAD = 80
STRIP_A = 64
STRIP_B = 64
STRIP_D = 32
STRIPS = STRIP_A + STRIP_B + STRIP_D
EPSILON = 1e-05
FAR = -1e30

NN = (((1,), (0,)), ((), ()))
NT = (((1,), (1,)), ((), ()))
TN = (((0,), (0,)), ((), ()))

LAT = ("x", "zh")
LON = ("zl", "y", "c")
DEPTH = ("zh", "zl")
CHIPS = ("x", "zh", "zl", "y")
EVERY = ("x", "zh", "zl", "y", "c")

A_CT = 0
A_O = A_CT + C2
A_DT = A_O + C2
A_N = A_DT + 3 * C2
A_HC = A_N + C2
A_NM = A_HC + C2
A_ALL = A_NM + 2 * C2


def routing():
    pack = np.zeros((STRIPS, TOK), np.float32)
    keep = np.zeros((TOK, TOK), np.float32)
    place = np.zeros((TOK, STRIPS), np.float32)
    half_a, half_o = WA // 2, WO // 2
    count = {"a": 0, "b": STRIP_A, "d": STRIP_A + STRIP_B}
    for r in range(ROWS):
        for c in range(COLS):
            gr, gc = r + half_a, c + half_o
            src = (gr % ROWS) * COLS + gc % COLS
            dst = r * COLS + c
            if gr < ROWS and gc < COLS:
                keep[dst, src] = 1
                continue
            kind = "a" if gc < COLS else ("b" if gr < ROWS else "d")
            slot = count[kind]
            count[kind] += 1
            pack[slot, src] = 1
            place[dst, slot] = 1
    patch = np.zeros((4 * M_PAD, TOK), np.float32)
    for part in range(4):
        for i in range(M_ROWS):
            for j in range(M_COLS):
                src = (2 * i + part % 2) * COLS + 2 * j + part // 2
                patch[part * M_PAD + i * M_COLS + j, src] = 1
    return [m.astype(jnp.bfloat16) for m in (pack, keep, place, patch)]


def dot(a, b, dims):
    return lax.dot_general(a, b, dims, preferred_element_type=F32)


def norm(field):
    values = field.astype(F32)
    centered = values - jnp.mean(values, axis=-1, keepdims=True)
    inverse = lax.rsqrt(jnp.mean(centered * centered, axis=-1, keepdims=True) + EPSILON)
    return centered * inverse, inverse


def norm_back(cotan, unit, inverse):
    cotan = cotan.astype(F32)
    along = jnp.mean(cotan * unit, axis=-1, keepdims=True)
    return (inverse * (cotan - jnp.mean(cotan, axis=-1, keepdims=True) - unit * along)).astype(BF16)


def add(a, b):
    return (a.astype(F32) + b.astype(F32)).astype(BF16)


def stacked(block):
    lane = lax.broadcasted_iota(jnp.int32, (1, PAIR), 1)
    first = jnp.where(lane < HDIM, 1.0, 0.0).astype(BF16)
    second = jnp.where(lane < HDIM, 0.0, 1.0).astype(BF16)
    return jnp.concatenate([block * first, block * second], axis=0)


def joined(both):
    size = both.shape[0] // 2
    lane = lax.broadcasted_iota(jnp.int32, (size, PAIR), 1)
    return jnp.where(lane < HDIM, both[:size], both[size:])


def softmax(queries, keys, bias):
    scores = dot(queries, keys, NT) * SCALE + bias
    raised = jnp.exp(scores - jnp.max(scores, axis=-1, keepdims=True))
    return raised * (1.0 / jnp.sum(raised, axis=-1, keepdims=True))


def attend(qkv_ref, o_ref, channels, spans, biases):
    for (start, size), bias in zip(spans, biases):
        rows = pl.ds(start, size)
        for pair in range(channels // PAIR):
            lanes = pair * PAIR
            q = stacked(qkv_ref[rows, lanes : lanes + PAIR])
            k = qkv_ref[rows, channels + lanes : channels + lanes + PAIR]
            v = qkv_ref[rows, 2 * channels + lanes : 2 * channels + lanes + PAIR]
            p = softmax(q, k, bias).astype(BF16)
            o_ref[rows, lanes : lanes + PAIR] = joined(dot(p, v, NN)).astype(BF16)


def attend_back(qkv_ref, do_ref, dqkv_ref, channels, spans, biases):
    for (start, size), bias in zip(spans, biases):
        rows = pl.ds(start, size)
        for pair in range(channels // PAIR):
            lanes = pair * PAIR
            q = stacked(qkv_ref[rows, lanes : lanes + PAIR])
            k = qkv_ref[rows, channels + lanes : channels + lanes + PAIR]
            v = qkv_ref[rows, 2 * channels + lanes : 2 * channels + lanes + PAIR]
            do = stacked(do_ref[rows, lanes : lanes + PAIR])
            p = softmax(q, k, bias)
            dp = dot(do, v, NT)
            inner = jnp.sum(p * dp, axis=-1, keepdims=True)
            ds = (p * (dp - inner) * SCALE).astype(BF16)
            dq = joined(dot(ds, k, NN))
            dk = dot(ds, q, TN)
            dv = dot(p.astype(BF16), do, TN)
            dqkv_ref[rows, lanes : lanes + PAIR] = dq.astype(BF16)
            dqkv_ref[rows, channels + lanes : channels + lanes + PAIR] = dk.astype(BF16)
            dqkv_ref[rows, 2 * channels + lanes : 2 * channels + lanes + PAIR] = dv.astype(BF16)


BANDS = [(0, BAND), (BAND, BAND)]


def band_biases(last_lat):
    def ids(dim, shape):
        token = lax.broadcasted_iota(jnp.int32, shape, dim)
        row = (token * 171) >> 12
        col = token - COLS * row
        return jnp.where(col >= WO, 1.0, 0.0), jnp.where(row >= WA // 2, 2.0, 0.0)

    win_q, half_q = ids(0, (BAND, BAND))
    win_k, half_k = ids(1, (BAND, BAND))
    plain = jnp.where(win_q == win_k, 0.0, FAR)
    plain = jnp.concatenate([plain, plain], axis=0)
    if last_lat is None:
        return [plain, plain]
    cut = jnp.where(win_q + half_q == win_k + half_k, 0.0, FAR)
    cut = jnp.concatenate([cut, cut], axis=0)
    return [plain, jnp.where(last_lat == 1, cut, plain)]


def first_forward(tok_ref, wqkv_ref, wo_ref, pack_ref, one_ref, strips_ref, qkv_ref, o_ref):
    unit, _ = norm(tok_ref[...])
    qkv_ref[...] = dot(unit.astype(BF16), wqkv_ref[...], NT).astype(BF16)
    attend(qkv_ref, o_ref, C1, BANDS, band_biases(None))
    out = dot(o_ref[...], wo_ref[...], NT).astype(BF16)
    one = add(tok_ref[...], out)
    one_ref[...] = one
    strips_ref[...] = dot(pack_ref[...], one, NN).astype(BF16)


def second_forward(
    last_ref, one_ref, in_a, in_b, in_d, wqkv_ref, wo_ref, keep_ref, place_ref,
    rolled_ref, own_ref, strips_ref, qkv_ref, o_ref,
):
    arrived = jnp.concatenate([in_a[...], in_b[...], in_d[...]], axis=0)
    rolled = (dot(keep_ref[...], one_ref[...], NN) + dot(place_ref[...], arrived, NN)).astype(BF16)
    rolled_ref[...] = rolled
    unit, _ = norm(rolled)
    qkv_ref[...] = dot(unit.astype(BF16), wqkv_ref[...], NT).astype(BF16)
    attend(qkv_ref, o_ref, C1, BANDS, band_biases(last_ref[0]))
    out = dot(o_ref[...], wo_ref[...], NT).astype(BF16)
    own_ref[...] = dot(keep_ref[...], out, TN).astype(BF16)
    strips_ref[...] = dot(place_ref[...], out, TN).astype(BF16)


def third_both(
    one_ref, own_ref, in_a, in_b, in_d, ct_ref, wm_ref, wqkv_ref, wo_ref, pack_ref, patch_ref,
    latent_ref, two_cot_ref, strips_ref, acts_ref,
    wide, qkv_ref, do_ref,
):
    arrived = jnp.concatenate([in_a[...], in_b[...], in_d[...]], axis=0)
    out_two = own_ref[...].astype(F32) + dot(pack_ref[...], arrived, TN)
    two = (one_ref[...].astype(F32) + out_two).astype(BF16)
    parts = dot(patch_ref[...], two, NN)
    merged = jnp.concatenate([parts[p * M_PAD : (p + 1) * M_PAD] for p in range(4)], axis=1)
    unit_m, inverse_m = norm(merged)
    acts_ref[:, A_NM : A_NM + 2 * C2] = unit_m.astype(BF16)
    hidden = dot(acts_ref[:, A_NM : A_NM + 2 * C2], wm_ref[...], NT).astype(BF16)
    unit_h, inverse_h = norm(hidden)
    acts_ref[:, A_N : A_N + C2] = unit_h.astype(BF16)
    qkv_ref[...] = dot(acts_ref[:, A_N : A_N + C2], wqkv_ref[...], NT).astype(BF16)
    key = lax.broadcasted_iota(jnp.int32, (2 * M_PAD, M_PAD), 1)
    bias = jnp.where(key < M_TOK, 0.0, FAR)
    span = [(0, M_PAD)]
    attend(qkv_ref, acts_ref.at[:, A_O : A_O + C2], C2, span, [bias])
    out = dot(acts_ref[:, A_O : A_O + C2], wo_ref[...], NT).astype(BF16)
    wide[...] = hidden.astype(F32) + out.astype(F32)
    for i in range(M_ROWS):
        latent_ref[i] = wide[i * M_COLS : (i + 1) * M_COLS, :].astype(BF16)
    wide[M_TOK:, :] = jnp.zeros((M_PAD - M_TOK, C2), F32)
    for i in range(M_ROWS):
        wide[i * M_COLS : (i + 1) * M_COLS, :] = ct_ref[i].astype(F32)
    cot = wide[...].astype(BF16)
    acts_ref[:, A_CT : A_CT + C2] = cot
    do_ref[...] = dot(cot, wo_ref[...], NN).astype(BF16)
    attend_back(qkv_ref, do_ref, acts_ref.at[:, A_DT : A_DT + 3 * C2], C2, span, [bias])
    dn = dot(acts_ref[:, A_DT : A_DT + 3 * C2], wqkv_ref[...], NN).astype(BF16)
    hidden_cot = add(cot, norm_back(dn, unit_h, inverse_h))
    acts_ref[:, A_HC : A_HC + C2] = hidden_cot
    dnm = dot(hidden_cot, wm_ref[...], NN).astype(BF16)
    merged_cot = norm_back(dnm, unit_m, inverse_m)
    two_cot = dot(patch_ref[0:M_PAD, :], merged_cot[:, 0:C1], TN)
    for p in range(1, 4):
        two_cot = two_cot + dot(
            patch_ref[p * M_PAD : (p + 1) * M_PAD, :], merged_cot[:, p * C1 : (p + 1) * C1], TN
        )
    two_cot = two_cot.astype(BF16)
    two_cot_ref[...] = two_cot
    strips_ref[...] = dot(pack_ref[...], two_cot, NN).astype(BF16)


T_ROWS = 96


def third_grads(core_ref, mine_ref, other_ref, out_ref):
    core = core_ref[0]
    half = C2 // 2

    def both(start, width):
        where = pl.ds(start, width)
        return jnp.concatenate([mine_ref[:, where], other_ref[:, where]], axis=0)

    n = both(pl.multiple_of(A_N + core * half, half), half)
    o = both(pl.multiple_of(A_O + core * half, half), half)
    nm = both(pl.multiple_of(A_NM + core * C2, C2), C2)
    for piece in range(8):
        step = 3 * C2 // 8
        grad = dot(both(A_DT + piece * step, step), n, TN).astype(BF16)
        out_ref[piece * 8 : piece * 8 + 8, 0:48] = grad.reshape(8, 48, half)
    for piece in range(4):
        step = C2 // 4
        chips = slice(piece * 16, piece * 16 + 16)
        grad = dot(both(A_CT + piece * step, step), o, TN).astype(BF16)
        out_ref[chips, 48:64] = grad.reshape(16, 16, half)
        hc = both(A_HC + piece * step, step)
        for side in range(2):
            grad = dot(hc, nm[:, side * half : side * half + half], TN).astype(BF16)
            out_ref[chips, 64 + 16 * side : 80 + 16 * side] = grad.reshape(16, 16, half)


S_ROWS = 32


def block_grads(core, dqkv_ref, unit_ref, cot, o_ref, keep_out, send_out):
    half = C1 // 2
    for ref, side in ((keep_out, core), (send_out, 1 - core)):
        where = pl.ds(pl.multiple_of(side * half, half), half)
        grad_qkv = dot(dqkv_ref[...], unit_ref[:, where], TN).reshape(64, 24, half)
        grad_out = dot(cot, o_ref[:, where], TN).reshape(64, 8, half)
        ref[...] = jnp.concatenate([grad_qkv, grad_out], axis=1).astype(BF16)


def second_back(
    last_ref, core_ref, two_cot_ref, in_a, in_b, in_d, rolled_ref, qkv_ref, o_ref, wqkv_ref, wo_ref,
    keep_ref, place_ref,
    own_ref, strips_ref, grad_keep, grad_send,
    do_ref, dqkv_ref, unit_ref,
):
    arrived = jnp.concatenate([in_a[...], in_b[...], in_d[...]], axis=0)
    cot = (dot(keep_ref[...], two_cot_ref[...], NN) + dot(place_ref[...], arrived, NN)).astype(BF16)
    unit, inverse = norm(rolled_ref[...])
    unit_ref[...] = unit.astype(BF16)
    do_ref[...] = dot(cot, wo_ref[...], NN).astype(BF16)
    attend_back(qkv_ref, do_ref, dqkv_ref, C1, BANDS, band_biases(last_ref[0]))
    dn = dot(dqkv_ref[...], wqkv_ref[...], NN).astype(BF16)
    rolled_cot = norm_back(dn, unit, inverse)
    own_ref[...] = dot(keep_ref[...], rolled_cot, TN).astype(BF16)
    strips_ref[...] = dot(place_ref[...], rolled_cot, TN).astype(BF16)
    block_grads(core_ref[0], dqkv_ref, unit_ref, cot, o_ref, grad_keep, grad_send)


def first_back(
    core_ref, two_cot_ref, own_ref, in_a, in_b, in_d, tok_ref, qkv_ref, o_ref, wqkv_ref, wo_ref, pack_ref,
    grad_ref, grad_keep, grad_send,
    do_ref, dqkv_ref, unit_ref,
):
    arrived = jnp.concatenate([in_a[...], in_b[...], in_d[...]], axis=0)
    back = own_ref[...].astype(F32) + dot(pack_ref[...], arrived, TN)
    cot = (two_cot_ref[...].astype(F32) + back).astype(BF16)
    unit, inverse = norm(tok_ref[...])
    unit_ref[...] = unit.astype(BF16)
    do_ref[...] = dot(cot, wo_ref[...], NN).astype(BF16)
    attend_back(qkv_ref, do_ref, dqkv_ref, C1, BANDS, band_biases(None))
    dn = dot(dqkv_ref[...], wqkv_ref[...], NN).astype(BF16)
    grad_ref[...] = add(cot, norm_back(dn, unit, inverse))
    block_grads(core_ref[0], dqkv_ref, unit_ref, cot, o_ref, grad_keep, grad_send)


VMEM = pl.BlockSpec(memory_space=pltpu.VMEM)
SMEM = pl.BlockSpec(memory_space=pltpu.SMEM)


def call(kernel, name, scalars, arrays, outs, scratch=(), flops=10**9, limit=56):
    moved = sum(a.size * a.dtype.itemsize for a in arrays)
    moved += sum(int(np.prod(s)) * 2 for s in outs)
    return pl.pallas_call(
        kernel,
        name=name,
        out_shape=[jax.ShapeDtypeStruct(s, BF16) for s in outs],
        in_specs=[SMEM] * len(scalars) + [VMEM] * len(arrays),
        out_specs=[VMEM] * len(outs),
        scratch_shapes=[pltpu.VMEM(s, d) for s, d in scratch],
        cost_estimate=pl.CostEstimate(flops=flops, bytes_accessed=moved, transcendentals=0),
        compiler_params=pltpu.CompilerParams(vmem_limit_bytes=limit * 2**20),
    )(*scalars, *arrays)


def send_strips(strips, step):
    lats, lons = 8, 16

    def route(lat_step, lon_step):
        return [
            (a * lons + o, (a + lat_step) % lats * lons + (o + lon_step) % lons)
            for a in range(lats)
            for o in range(lons)
        ]

    a = lax.ppermute(strips[:STRIP_A], EVERY, route(step, 0))
    b = lax.ppermute(strips[STRIP_A : STRIP_A + STRIP_B], EVERY, route(0, step))
    d = lax.ppermute(strips[STRIP_A + STRIP_B :], EVERY, route(step, step))
    return a, b, d


def other_core(block):
    return lax.ppermute(block, "c", [(0, 1), (1, 0)])


def over_chips(block):
    block = lax.psum_scatter(block, "x", scatter_dimension=0, tiled=True)
    block = lax.psum_scatter(block, DEPTH, scatter_dimension=0, tiled=True)
    return lax.psum_scatter(block, "y", scatter_dimension=0, tiled=True)[0]


def exchange_chips(block):
    block = lax.all_to_all(block, CHIPS, split_axis=0, concat_axis=0, tiled=True)
    return jnp.sum(block.astype(F32), axis=0)


def on_device(
    tokens, qkv_first, out_first, qkv_second, out_second, merge_weight, qkv_third, out_third, cotangent
):
    pack, keep, place, patch = (jnp.asarray(m) for m in routing())
    core = lax.axis_index("c").astype(jnp.int32)
    core_s = core.reshape(1)
    last = (lax.axis_index(LAT) == 7).astype(jnp.int32).reshape(1)
    tok = tokens.reshape(TOK, C1)
    wide, slim = (TOK, 3 * C1), (TOK, C1)
    one, strips, qkv1, o1 = call(
        first_forward, "first_forward", [], [tok, qkv_first, out_first, pack],
        [slim, (STRIPS, C1), wide, slim],
    )
    arrived = send_strips(strips, -1)
    rolled, own, strips, qkv2, o2 = call(
        second_forward, "second_forward", [last], [one, *arrived, qkv_second, out_second, keep, place],
        [slim, slim, (STRIPS, C1), wide, slim],
    )
    arrived = send_strips(strips, 1)
    latent, two_cot, strips, acts = call(
        third_both, "third_both", [],
        [one, own, *arrived, cotangent[0], merge_weight, qkv_third, out_third, pack, patch],
        [(M_ROWS, M_COLS, C2), slim, (STRIPS, C1), (M_PAD, A_ALL)],
        [((M_PAD, C2), F32), ((M_PAD, 3 * C2), BF16), ((M_PAD, C2), BF16)],
    )
    arrived = send_strips(strips, -1)
    acts_other = other_core(acts)
    (grads_t,) = call(third_grads, "third_grads", [core_s], [acts, acts_other], [(64, T_ROWS, C2 // 2)])
    share_t = over_chips(grads_t)
    back_scratch = [(slim, BF16), (wide, BF16), (slim, BF16)]
    half = (64, S_ROWS, C1 // 2)
    own, strips, keep2, send2 = call(
        second_back, "second_back", [last, core_s],
        [two_cot, *arrived, rolled, qkv2, o2, qkv_second, out_second, keep, place],
        [slim, (STRIPS, C1), half, half], back_scratch,
    )
    arrived = send_strips(strips, 1)
    tokens_grad, keep1, send1 = call(
        first_back, "first_back", [core_s],
        [two_cot, own, *arrived, tok, qkv1, o1, qkv_first, out_first, pack],
        [slim, half, half], back_scratch,
    )
    share_s = exchange_chips(add(keep2, other_core(send2)))
    share_f = exchange_chips(add(keep1, other_core(send1)))

    share_t = share_t.astype(F32)

    def halves(share, rows, start):
        block = share[start : start + 2 * rows].reshape(2, rows, -1)
        return block

    t_q = halves(share_t, 24, 0)
    t_o = halves(share_t, 8, 48)
    t_m = jnp.concatenate([halves(share_t, 8, 64), halves(share_t, 8, 80)], axis=2)
    s_q, s_o = halves(share_s, 12, 0), halves(share_s, 4, 24)
    f_q, f_o = halves(share_f, 12, 0), halves(share_f, 4, 24)
    shares = [f_q, f_o, s_q, s_o, t_m, t_q, t_o]
    flat = jnp.concatenate([s.reshape(2, -1, 256) for s in shares], axis=1).astype(BF16)
    mine = lax.dynamic_index_in_dim(flat, core, 0, keepdims=False)
    given = other_core(lax.dynamic_index_in_dim(flat, 1 - core, 0, keepdims=False))
    outs, at = [], 0
    for s in shares:
        rows, width = s.shape[1:]
        count = rows * width // 256
        low = mine[at : at + count].reshape(rows, width)
        high = given[at : at + count].reshape(rows, width)
        at += count
        outs.append(
            jnp.where(
                core == 0,
                jnp.concatenate([low, high], axis=1),
                jnp.concatenate([high, low], axis=1),
            ).astype(F32)
        )
    return (latent[None], tokens_grad.reshape(tokens.shape), *outs)


def solution(mesh):
    split = Mesh(mesh.devices.reshape(4, 2, 2, 4, 2), EVERY)
    grid = P(None, LAT, LON, None)
    return jax.shard_map(
        on_device,
        mesh=split,
        in_specs=(grid,) + (P(),) * 7 + (grid,),
        out_specs=(grid, grid) + (P(EVERY, None),) * 7,
        check_vma=False,
    )
```

time: 1940 us -> 253 us (0.13)
  waiting for transfers between devices: 1010 us -> 132 us
  blocking collectives: 365 us -> 0 us
  local copies, waits for them, and re-layouts: 174 us -> 10.6 us
  starting transfers between devices: 183 us -> 32.5 us
  matrix products: 130 us -> 0 us
  Pallas kernels: 0 us -> 55.4 us
  other arithmetic: 47.1 us -> 6.31 us
    reduce_scatter x2 -> x3, waiting for transfers between devices: 868 us -> 69 us  [the longest x1 61.6 us: over_chips(): block = lax.psum_scatter(block, 'x', scatter_dimension=0, tiled=True)]
    unnamed x1 -> x0, blocking collectives: 365 us -> none
    unnamed x66 -> x0, starting transfers between devices: 166 us -> none
    dot_general x43 -> x0, matrix products: 124 us -> none  [the longest x7 22.9 us: grad_weight(): lax.dot_general(cotan, rows, (((0,), (0,)), ((), ())), preferred_element_...]
    unnamed x70 -> x3, waiting for transfers between devices: 108 us -> 0.69 us
    unnamed x317 -> x32, local copies, waits for them, and re-layouts: 103 us -> 3.78 us
    pallas_call x0 -> x6, Pallas kernels: none -> 55.4 us  [call(): pl.pallas_call(kernel, name=name, out_shape=[jax.ShapeDtypeStruct(s, BF16...]
    all_to_all x0 -> x2, waiting for transfers between devices: none -> 34.4 us  [exchange_chips(): lax.all_to_all(block, CHIPS, split_axis=0, concat_axis=0, tiled=True)]
  transfers between devices with their start and end apart: 76 -> 21, of which waited for: 11 -> 10; matrix products, arithmetic and copies ran while one was open for 27% -> 3% of each run, Pallas kernels for 0% -> 8%
where the time goes in v1:
time: 253 us; the launch traced here: 251 us
  waiting for transfers between devices  132 us (52%)
  Pallas kernels  55.4 us (22%)
  starting transfers between devices  32.5 us (13%)
  between operations  14.1 us (6%)
  local copies, waits for them, and re-layouts  10.6 us (4%)
  other arithmetic  6.31 us (2%)
    reduce_scatter x1, waiting for transfers between devices, over_chips(): block = lax.psum_scatter(block, 'x', scatter_dimension=0, tiled=True)  61.6 us
    pallas_call x6, Pallas kernels, call(): pl.pallas_call(kernel, name=name, out_shape=[jax.ShapeDtypeStruct(s, BF16...  55.4 us
    all_to_all x2, waiting for transfers between devices, exchange_chips(): lax.all_to_all(block, CHIPS, split_axis=0, concat_axis=0, tiled=True)  34.4 us
    ppermute x4, waiting for transfers between devices, send_strips(): d = lax.ppermute(strips[STRIP_A + STRIP_B:], EVERY, route(step, step))  23.4 us
    ppermute x4, starting transfers between devices, send_strips(): a = lax.ppermute(strips[:STRIP_A], EVERY, route(step, 0))  12.9 us
    all_to_all x2, starting transfers between devices, exchange_chips(): lax.all_to_all(block, CHIPS, split_axis=0, concat_axis=0, tiled=True)  9.9 us
    reduce_scatter x1, waiting for transfers between devices, over_chips(): return lax.psum_scatter(block, 'y', scatter_dimension=0, tiled=True)[0]  7.35 us
  transfers between devices with their start and end apart: 21, of which 10 were waited for; matrix products, arithmetic and copies ran while one was open for 3% of the time, Pallas kernels for 8%

profile of v1, /device:TPU:0, one launch (start us, length us, event | category | flops | bytes accessed | tf_op | source)
XLA Modules:
  0.0 251.0 jit_solution(13938567109055903931)
XLA Ops:
  7.2 5.2 %first_forward.1 = (bf16[288,512]{1,0:T(8,128)(2,1)}, bf16[160,512]{1,0:T(8,128)(2,1)}, bf16[288,1536]{1,0:T(8,128)(2,1)}, bf16[288,512]{1,0:T(8,128)(2,1)}) custom-call(bf16[288,512]{1,0:T(8,128)(2,1)} %bitcast.20, bf16[1536,512]{1,0:T(8,128)(2,1)} %wqkv_ref.9, bf16[512,512]{1,0:T(8,128)(2,1)} %wo_ref.9, bf16[160,288]{1,0:T(8,128)(2,1)} %constant.40.clone.pack_ref), custom_call_target="tpu_custom_call" | custom-call | flops 1000000000 | bytes 4122624 | tf_op jit(solution)/shard_map/first_forward/pallas_call | solution.py:331
  12.4 0.9 fusion.10
  13.3 6.2 %collective-permute-start = (bf16[64,512]{1,0:T(8,128)(2,1)S(1)}, bf16[64,512]{1,0:T(8,128)(2,1)S(1)}, u32[]{:S(2)}, u32[]{:S(2)}) collective-permute-start(bf16[64,512]{1,0:T(8,128)(2,1)S(1)} %get-tuple-element.56), channel_id=1, source_target_pairs={{0,112},{1,113},{2,114},{3,115},{4,116},{5,117},{6,118},{7,119},{8... | collective-permute-start | bytes 196616 | tf_op jit(solution)/shard_map/ppermute | solution.py:353
  19.5 2.6 %collective-permute-start.1 = (bf16[64,512]{1,0:T(8,128)(2,1)S(1)}, bf16[64,512]{1,0:T(8,128)(2,1)S(1)}, u32[]{:S(2)}, u32[]{:S(2)}) collective-permute-start(bf16[64,512]{1,0:T(8,128)(2,1)S(1)} %get-tuple-element.55), channel_id=1, source_target_pairs={{0,15},{1,0},{2,1},{3,2},{4,3},{5,4},{6,5},{7,6},{8,7},{9,8},{10,9... | collective-permute-start | bytes 196616 | tf_op jit(solution)/shard_map/ppermute | solution.py:354
  23.6 4.2 %collective-permute-done.2.in_d = bf16[32,512]{1,0:T(8,128)(2,1)S(1)} collective-permute-done((bf16[32,512]{1,0:T(8,128)(2,1)S(1)}, bf16[32,512]{1,0:T(8,128)(2,1)S(1)}, u32[]{:S(2)}, u32[]{:S(2)}) %collective-permute-start.2) | collective-permute-done | bytes 32800 | tf_op jit(solution)/shard_map/ppermute | solution.py:355
  28.4 5.5 %second_forward.1 = (bf16[288,512]{1,0:T(8,128)(2,1)}, bf16[288,512]{1,0:T(8,128)(2,1)}, bf16[160,512]{1,0:T(8,128)(2,1)}, bf16[288,1536]{1,0:T(8,128)(2,1)}, bf16[288,512]{1,0:T(8,128)(2,1)}) custom-call(s32[1]{0:T(128)} %bitcast.1.last_ref, bf16[288,512]{1,0:T(8,128)(2,1)} %get-tuple-element.29.one_ref, bf16[64,512]{1,0:T(8,128)(2,1)} %copy-done.13, ...), custom_call_target="tpu_custom_call" | custom-call | flops 1000000000 | bytes 4747264 | tf_op jit(solution)/shard_map/second_forward/pallas_call | solution.py:331
  34.0 0.9 fusion.9
  36.6 8.7 %collective-permute-done.5.in_d = bf16[32,512]{1,0:T(8,128)(2,1)S(1)} collective-permute-done((bf16[32,512]{1,0:T(8,128)(2,1)S(1)}, bf16[32,512]{1,0:T(8,128)(2,1)S(1)}, u32[]{:S(2)}, u32[]{:S(2)}) %collective-permute-start.5) | collective-permute-done | bytes 32800 | tf_op jit(solution)/shard_map/ppermute | solution.py:355
  46.0 17.9 %third_both.1 = (bf16[6,12,1024]{2,1,0:T(8,128)(2,1)}, bf16[288,512]{1,0:T(8,128)(2,1)}, bf16[160,512]{1,0:T(8,128)(2,1)}, bf16[80,9216]{1,0:T(8,128)(2,1)}) custom-call(bf16[288,512]{1,0:T(8,128)(2,1)} %get-tuple-element.29.one_ref, bf16[288,512]{1,0:T(8,128)(2,1)} %get-tuple-element.31.own_ref, bf16[64,512]{1,0:T(8,128)(2,1)} %copy-done.6, ...), custom_call_target="tpu_custom_call" | custom-call | flops 1000000000 | bytes 15841280 | tf_op jit(solution)/shard_map/third_both/pallas_call | solution.py:331
  63.9 3.5 %collective-permute-done.14.other_ref = bf16[80,9216]{1,0:T(8,128)(2,1)S(1)} collective-permute-done((bf16[80,9216]{1,0:T(8,128)(2,1)}, bf16[80,9216]{1,0:T(8,128)(2,1)S(1)}, u32[]{:S(2)}, u32[]{:S(2)}) %collective-permute-start.14) | collective-permute-done | bytes 1474592 | tf_op jit(solution)/shard_map/ppermute | solution.py:360
  67.4 1.2 copy-done
  68.6 6.4 %third_grads.1 = bf16[64,96,512]{2,1,0:T(8,128)(2,1)} custom-call(s32[1]{0:T(128)} %bitcast.4.core_ref, bf16[80,9216]{1,0:T(8,128)(2,1)} %get-tuple-element.48.mine_ref, bf16[80,9216]{1,0:T(8,128)(2,1)} %copy-done), custom_call_target="tpu_custom_call" | custom-call | flops 1000000000 | bytes 9240576 | tf_op jit(solution)/shard_map/third_grads/pallas_call | solution.py:331
  75.0 61.6 %reduce-scatter.4.cloned.1.call-done = bf16[16,96,512]{2,1,0:T(8,128)(2,1)} async-done(((bf16[64,96,512]{2,1,0:T(8,128)(2,1)}), bf16[16,96,512]{2,1,0:T(8,128)(2,1)}) %reduce-scatter.4.cloned.1.call-update) | async-done | bytes 1572880 | tf_op jit(solution)/shard_map/reduce_scatter | solution.py:364
  136.7 3.5 %collective-permute-start.6 = (bf16[64,512]{1,0:T(8,128)(2,1)S(1)}, bf16[64,512]{1,0:T(8,128)(2,1)S(1)}, u32[]{:S(2)}, u32[]{:S(2)}) collective-permute-start(bf16[64,512]{1,0:T(8,128)(2,1)S(1)} %get-tuple-element.52), channel_id=1, source_target_pairs={{0,112},{1,113},{2,114},{3,115},{4,116},{5,117},{6,118},{7,119},{8... | collective-permute-start | bytes 196616 | tf_op jit(solution)/shard_map/ppermute | solution.py:353
  140.2 2.1 collective-permute-start.7
  142.3 1.3 collective-permute-start.8
  143.6 3.5 %collective-permute-done.8.in_d = bf16[32,512]{1,0:T(8,128)(2,1)S(1)} collective-permute-done((bf16[32,512]{1,0:T(8,128)(2,1)S(1)}, bf16[32,512]{1,0:T(8,128)(2,1)S(1)}, u32[]{:S(2)}, u32[]{:S(2)}) %collective-permute-start.8) | collective-permute-done | bytes 32800 | tf_op jit(solution)/shard_map/ppermute | solution.py:355
  147.8 10.4 %second_back.1 = (bf16[288,512]{1,0:T(8,128)(2,1)}, bf16[160,512]{1,0:T(8,128)(2,1)}, bf16[64,32,256]{2,1,0:T(8,128)(2,1)}, bf16[64,32,256]{2,1,0:T(8,128)(2,1)}) custom-call(s32[1]{0:T(128)} %bitcast.1.last_ref, s32[1]{0:T(128)} %bitcast.4.core_ref, bf16[288,512]{1,0:T(8,128)(2,1)} %get-tuple-element.34.two_cot_ref, bf16[64,512]{1,0:T(8,128)(2,1)} %copy-done.4, ...), custom_call_target="tpu_custom_call" | custom-call | flops 1000000000 | bytes 6844416 | tf_op jit(solution)/shard_map/second_back/pallas_call | solution.py:331
  158.2 0.9 fusion.7
  159.1 2.9 %collective-permute-start.9 = (bf16[64,512]{1,0:T(8,128)(2,1)S(1)}, bf16[64,512]{1,0:T(8,128)(2,1)S(1)}, u32[]{:S(2)}, u32[]{:S(2)}) collective-permute-start(bf16[64,512]{1,0:T(8,128)(2,1)S(1)} %get-tuple-element.50), channel_id=1, source_target_pairs={{0,16},{1,17},{2,18},{3,19},{4,20},{5,21},{6,22},{7,23},{8,24},{9,... | collective-permute-start | bytes 196616 | tf_op jit(solution)/shard_map/ppermute | solution.py:353
  163.0 1.9 collective-permute-start.11
  164.9 6.9 %collective-permute-done.11.in_d = bf16[32,512]{1,0:T(8,128)(2,1)S(1)} collective-permute-done((bf16[32,512]{1,0:T(8,128)(2,1)S(1)}, bf16[32,512]{1,0:T(8,128)(2,1)S(1)}, u32[]{:S(2)}, u32[]{:S(2)}) %collective-permute-start.11) | collective-permute-done | bytes 32800 | tf_op jit(solution)/shard_map/ppermute | solution.py:355
  172.4 10.0 %first_back.1 = (bf16[288,512]{1,0:T(8,128)(2,1)}, bf16[64,32,256]{2,1,0:T(8,128)(2,1)}, bf16[64,32,256]{2,1,0:T(8,128)(2,1)}) custom-call(s32[1]{0:T(128)} %bitcast.4.core_ref, bf16[288,512]{1,0:T(8,128)(2,1)} %get-tuple-element.34.two_cot_ref, bf16[288,512]{1,0:T(8,128)(2,1)} %get-tuple-element.39.own_ref, bf16[64,512]{1,0:T(8,128)(2,1)} %copy-done.5, ...), custom_call_target="tpu_custom_call" | custom-call | flops 1000000000 | bytes 6809600 | tf_op jit(solution)/shard_map/first_back/pallas_call | solution.py:331
  182.4 1.4 add_convert_fusion
  183.8 5.1 %all-to-all-start.1 = ((bf16[64,32,256]{2,1,0:T(8,128)(2,1)}), bf16[64,32,256]{2,1,0:T(8,128)(2,1)S(1)}, u32[]{:S(2)}, u32[]{:S(2)}) async-start(bf16[64,32,256]{2,1,0:T(8,128)(2,1)} %add_convert_fusion), calls=%async_computation.1 | async-start | bytes 2097152 | tf_op jit(solution)/shard_map/all_to_all | solution.py:370
  189.0 1.4 add_convert_fusion.1
  190.4 17.6 %all-to-all-done.1 = bf16[64,32,256]{2,1,0:T(8,128)(2,1)S(1)} async-done(((bf16[64,32,256]{2,1,0:T(8,128)(2,1)}), bf16[64,32,256]{2,1,0:T(8,128)(2,1)S(1)}, u32[]{:S(2)}, u32[]{:S(2)}) %all-to-all-start.1) | async-done | bytes 1048608 | tf_op jit(solution)/shard_map/all_to_all | solution.py:370
  208.0 4.8 %all-to-all-start = ((bf16[64,32,256]{2,1,0:T(8,128)(2,1)}), bf16[64,32,256]{2,1,0:T(8,128)(2,1)S(1)}, u32[]{:S(2)}, u32[]{:S(2)}) async-start(bf16[64,32,256]{2,1,0:T(8,128)(2,1)} %add_convert_fusion.1), calls=%async_computation | async-start | bytes 2097152 | tf_op jit(solution)/shard_map/all_to_all | solution.py:370
  213.7 16.9 %all-to-all-done = bf16[64,32,256]{2,1,0:T(8,128)(2,1)S(1)} async-done(((bf16[64,32,256]{2,1,0:T(8,128)(2,1)}), bf16[64,32,256]{2,1,0:T(8,128)(2,1)S(1)}, u32[]{:S(2)}, u32[]{:S(2)}) %all-to-all-start) | async-done | bytes 1048608 | tf_op jit(solution)/shard_map/all_to_all | solution.py:370
  230.8 7.4 %reduce-scatter.8.cloned.1.call-done = bf16[1,96,512]{2,1,0:T(8,128)(2,1)} async-done(((bf16[4,96,512]{2,1,0:T(8,128)(2,1)}), bf16[1,96,512]{2,1,0:T(8,128)(2,1)}) %reduce-scatter.8.cloned.1.call-update) | async-done | bytes 98320 | tf_op jit(solution)/shard_map/reduce_scatter | solution.py:366
  238.9 0.8 slice.173
  240.1 1.1 collective-permute-done.15
  (100 shorter events, 12.3 us)
Async XLA Ops:
  7.2 129.5 %reduce-scatter.4.cloned.1.call-start = ((), (), s32[]{:S(2)}) async-start(), calls=%async_computation.5 | async-start | bytes 7864320 | tf_op jit(solution)/shard_map/reduce_scatter | solution.py:364
  13.3 14.5 %collective-permute-start = (bf16[64,512]{1,0:T(8,128)(2,1)S(1)}, bf16[64,512]{1,0:T(8,128)(2,1)S(1)}, u32[]{:S(2)}, u32[]{:S(2)}) collective-permute-start(bf16[64,512]{1,0:T(8,128)(2,1)S(1)} %get-tuple-element.56), channel_id=1, source_target_pairs={{0,112},{1,113},{2,114},{3,115},{4,116},{5,117},{6,118},{7,119},{8... | collective-permute-start | bytes 196616 | tf_op jit(solution)/shard_map/ppermute | solution.py:353
  19.5 8.2 %collective-permute-start.1 = (bf16[64,512]{1,0:T(8,128)(2,1)S(1)}, bf16[64,512]{1,0:T(8,128)(2,1)S(1)}, u32[]{:S(2)}, u32[]{:S(2)}) collective-permute-start(bf16[64,512]{1,0:T(8,128)(2,1)S(1)} %get-tuple-element.55), channel_id=1, source_target_pairs={{0,15},{1,0},{2,1},{3,2},{4,3},{5,4},{6,5},{7,6},{8,7},{9,8},{10,9... | collective-permute-start | bytes 196616 | tf_op jit(solution)/shard_map/ppermute | solution.py:354
  22.9 4.8 %collective-permute-start.2 = (bf16[32,512]{1,0:T(8,128)(2,1)S(1)}, bf16[32,512]{1,0:T(8,128)(2,1)S(1)}, u32[]{:S(2)}, u32[]{:S(2)}) collective-permute-start(bf16[32,512]{1,0:T(8,128)(2,1)S(1)} %slice.131), channel_id=1, source_target_pairs={{0,127},{1,112},{2,113},{3,114},{4,115},{5,116},{6,117},{7,118},{8... | collective-permute-start | bytes 98312 | tf_op jit(solution)/shard_map/ppermute | solution.py:355
  27.8 0.6 copy-start.13
  27.8 0.6 copy-start.14
  34.8 10.5 %collective-permute-start.3 = (bf16[64,512]{1,0:T(8,128)(2,1)S(1)}, bf16[64,512]{1,0:T(8,128)(2,1)S(1)}, u32[]{:S(2)}, u32[]{:S(2)}) collective-permute-start(bf16[64,512]{1,0:T(8,128)(2,1)S(1)} %get-tuple-element.54), channel_id=1, source_target_pairs={{0,16},{1,17},{2,18},{3,19},{4,20},{5,21},{6,22},{7,23},{8,24},{9,... | collective-permute-start | bytes 196616 | tf_op jit(solution)/shard_map/ppermute | solution.py:353
  35.1 10.3 %collective-permute-start.4 = (bf16[64,512]{1,0:T(8,128)(2,1)S(1)}, bf16[64,512]{1,0:T(8,128)(2,1)S(1)}, u32[]{:S(2)}, u32[]{:S(2)}) collective-permute-start(bf16[64,512]{1,0:T(8,128)(2,1)S(1)} %get-tuple-element.53), channel_id=1, source_target_pairs={{0,1},{1,2},{2,3},{3,4},{4,5},{5,6},{6,7},{7,8},{8,9},{9,10},{10,1... | collective-permute-start | bytes 196616 | tf_op jit(solution)/shard_map/ppermute | solution.py:354
  35.8 9.5 %collective-permute-start.5 = (bf16[32,512]{1,0:T(8,128)(2,1)S(1)}, bf16[32,512]{1,0:T(8,128)(2,1)S(1)}, u32[]{:S(2)}, u32[]{:S(2)}) collective-permute-start(bf16[32,512]{1,0:T(8,128)(2,1)S(1)} %slice.134), channel_id=1, source_target_pairs={{0,17},{1,18},{2,19},{3,20},{4,21},{5,22},{6,23},{7,24},{8,25},{9,... | collective-permute-start | bytes 98312 | tf_op jit(solution)/shard_map/ppermute | solution.py:355
  45.3 0.6 copy-start.6
  45.3 0.6 copy-start.9
  63.9 3.5 %collective-permute-start.14 = (bf16[80,9216]{1,0:T(8,128)(2,1)}, bf16[80,9216]{1,0:T(8,128)(2,1)S(1)}, u32[]{:S(2)}, u32[]{:S(2)}) collective-permute-start(bf16[80,9216]{1,0:T(8,128)(2,1)} %get-tuple-element.48.mine_ref), channel_id=1, source_target_pairs={{0,1},{1,0},{2,3},{3,2},{4,5},{5,4},{6,7},{7,6},{8,9},{9,8},{10,11... | collective-permute-start | bytes 4423688 | tf_op jit(solution)/shard_map/ppermute | solution.py:360
  67.4 1.2 copy-start
  74.9 61.7 %copy-start.3 = (bf16[160,512]{1,0:T(8,128)(2,1)S(1)}, bf16[160,512]{1,0:T(8,128)(2,1)}, u32[]{:S(2)}) copy-start(bf16[160,512]{1,0:T(8,128)(2,1)} %get-tuple-element.35) | copy-start | bytes 491524
  75.0 137.9 %reduce-scatter.6.cloned.1.call-start = ((), (), s32[]{:S(2)}) async-start(), calls=%async_computation.6 | async-start | bytes 1966080 | tf_op jit(solution)/shard_map/reduce_scatter | solution.py:365
  136.7 10.5 %collective-permute-start.6 = (bf16[64,512]{1,0:T(8,128)(2,1)S(1)}, bf16[64,512]{1,0:T(8,128)(2,1)S(1)}, u32[]{:S(2)}, u32[]{:S(2)}) collective-permute-start(bf16[64,512]{1,0:T(8,128)(2,1)S(1)} %get-tuple-element.52), channel_id=1, source_target_pairs={{0,112},{1,113},{2,114},{3,115},{4,116},{5,117},{6,118},{7,119},{8... | collective-permute-start | bytes 196616 | tf_op jit(solution)/shard_map/ppermute | solution.py:353
  140.2 6.9 %collective-permute-start.7 = (bf16[64,512]{1,0:T(8,128)(2,1)S(1)}, bf16[64,512]{1,0:T(8,128)(2,1)S(1)}, u32[]{:S(2)}, u32[]{:S(2)}) collective-permute-start(bf16[64,512]{1,0:T(8,128)(2,1)S(1)} %get-tuple-element.51), channel_id=1, source_target_pairs={{0,15},{1,0},{2,1},{3,2},{4,3},{5,4},{6,5},{7,6},{8,7},{9,8},{10,9... | collective-permute-start | bytes 196616 | tf_op jit(solution)/shard_map/ppermute | solution.py:354
  142.3 4.8 %collective-permute-start.8 = (bf16[32,512]{1,0:T(8,128)(2,1)S(1)}, bf16[32,512]{1,0:T(8,128)(2,1)S(1)}, u32[]{:S(2)}, u32[]{:S(2)}) collective-permute-start(bf16[32,512]{1,0:T(8,128)(2,1)S(1)} %slice.137), channel_id=1, source_target_pairs={{0,127},{1,112},{2,113},{3,114},{4,115},{5,116},{6,117},{7,118},{8... | collective-permute-start | bytes 98312 | tf_op jit(solution)/shard_map/ppermute | solution.py:355
  147.1 0.6 copy-start.4
  147.2 0.6 copy-start.7
  158.2 24.2 %collective-permute-start.13 = (bf16[64,32,256]{2,1,0:T(8,128)(2,1)}, bf16[64,32,256]{2,1,0:T(8,128)(2,1)S(1)}, u32[]{:S(2)}, u32[]{:S(2)}) collective-permute-start(bf16[64,32,256]{2,1,0:T(8,128)(2,1)} %get-tuple-element.47), channel_id=1, source_target_pairs={{0,1},{1,0},{2,3},{3,2},{4,5},{5,4},{6,7},{7,6},{8,9},{9,8},{10,11... | collective-permute-start | bytes 3145736 | tf_op jit(solution)/shard_map/ppermute | solution.py:360
  159.1 12.7 %collective-permute-start.9 = (bf16[64,512]{1,0:T(8,128)(2,1)S(1)}, bf16[64,512]{1,0:T(8,128)(2,1)S(1)}, u32[]{:S(2)}, u32[]{:S(2)}) collective-permute-start(bf16[64,512]{1,0:T(8,128)(2,1)S(1)} %get-tuple-element.50), channel_id=1, source_target_pairs={{0,16},{1,17},{2,18},{3,19},{4,20},{5,21},{6,22},{7,23},{8,24},{9,... | collective-permute-start | bytes 196616 | tf_op jit(solution)/shard_map/ppermute | solution.py:353
  162.0 9.8 %collective-permute-start.10 = (bf16[64,512]{1,0:T(8,128)(2,1)S(1)}, bf16[64,512]{1,0:T(8,128)(2,1)S(1)}, u32[]{:S(2)}, u32[]{:S(2)}) collective-permute-start(bf16[64,512]{1,0:T(8,128)(2,1)S(1)} %get-tuple-element.49), channel_id=1, source_target_pairs={{0,1},{1,2},{2,3},{3,4},{4,5},{5,6},{6,7},{7,8},{8,9},{9,10},{10,1... | collective-permute-start | bytes 196616 | tf_op jit(solution)/shard_map/ppermute | solution.py:354
  163.0 8.8 %collective-permute-start.11 = (bf16[32,512]{1,0:T(8,128)(2,1)S(1)}, bf16[32,512]{1,0:T(8,128)(2,1)S(1)}, u32[]{:S(2)}, u32[]{:S(2)}) collective-permute-start(bf16[32,512]{1,0:T(8,128)(2,1)S(1)} %slice.140), channel_id=1, source_target_pairs={{0,17},{1,18},{2,19},{3,20},{4,21},{5,22},{6,23},{7,24},{8,25},{9,... | collective-permute-start | bytes 98312 | tf_op jit(solution)/shard_map/ppermute | solution.py:355
  171.8 0.6 copy-start.8
  172.4 10.0 %copy-start.1 = (bf16[64,32,256]{2,1,0:T(8,128)(2,1)S(1)}, bf16[64,32,256]{2,1,0:T(8,128)(2,1)}, u32[]{:S(2)}) copy-start(bf16[64,32,256]{2,1,0:T(8,128)(2,1)} %get-tuple-element.46) | copy-start | bytes 3145732
  182.4 6.5 %collective-permute-start.12 = (bf16[64,32,256]{2,1,0:T(8,128)(2,1)}, bf16[64,32,256]{2,1,0:T(8,128)(2,1)S(1)}, u32[]{:S(2)}, u32[]{:S(2)}) collective-permute-start(bf16[64,32,256]{2,1,0:T(8,128)(2,1)} %get-tuple-element.45), channel_id=1, source_target_pairs={{0,1},{1,0},{2,3},{3,2},{4,5},{5,4},{6,7},{7,6},{8,9},{9,8},{10,11... | collective-permute-start | bytes 3145736 | tf_op jit(solution)/shard_map/ppermute | solution.py:360
  182.4 6.5 %copy-start.2 = (bf16[64,32,256]{2,1,0:T(8,128)(2,1)S(1)}, bf16[64,32,256]{2,1,0:T(8,128)(2,1)}, u32[]{:S(2)}) copy-start(bf16[64,32,256]{2,1,0:T(8,128)(2,1)} %get-tuple-element.44) | copy-start | bytes 3145732
  183.8 24.1 %all-to-all-start.1 = ((bf16[64,32,256]{2,1,0:T(8,128)(2,1)}), bf16[64,32,256]{2,1,0:T(8,128)(2,1)S(1)}, u32[]{:S(2)}, u32[]{:S(2)}) async-start(bf16[64,32,256]{2,1,0:T(8,128)(2,1)} %add_convert_fusion), calls=%async_computation.1 | async-start | bytes 2097152 | tf_op jit(solution)/shard_map/all_to_all | solution.py:370
  208.0 22.6 %all-to-all-start = ((bf16[64,32,256]{2,1,0:T(8,128)(2,1)}), bf16[64,32,256]{2,1,0:T(8,128)(2,1)S(1)}, u32[]{:S(2)}, u32[]{:S(2)}) async-start(bf16[64,32,256]{2,1,0:T(8,128)(2,1)} %add_convert_fusion.1), calls=%async_computation | async-start | bytes 2097152 | tf_op jit(solution)/shard_map/all_to_all | solution.py:370
  212.8 25.4 %reduce-scatter.8.cloned.1.call-start = ((), (), s32[]{:S(2)}) async-start(), calls=%async_computation.7 | async-start | bytes 491520 | tf_op jit(solution)/shard_map/reduce_scatter | solution.py:366
  239.9 1.3 collective-permute-start.15
  (5 other events, 3.1 us)
Sparse Core Ops, SparseCore 0:
  75.1 61.5 reduce-scatter.3
  139.0 25.5 reduce-scatter.5
  216.0 22.1 reduce-scatter.7
